TPU v7x, 256 devices: a whole 4x4x8 slice. The times are simulated.
256 devices in a mesh: dom: 16 (over z, core), tile: 16 (over x, y).
Axes of the slice: x: 4, y: 4, z: 8, core: 2. Of those that a mesh axis runs over, the one named last changes fastest.
Arguments:
- members: float32 [256, 4, 128, 384], P('dom', None, 'tile'), may hold values from -6 to 6
- noise: float32 [2, 256, 4, 128, 384], P(None, 'dom', None, 'tile'), may hold values from -4 to 4
- courant: float32 [2, 128, 384], P(None, 'tile'), may hold values from -0.35 to 0.35
- diffusion: float32 [4, 128, 384], P(None, 'tile'), may hold values from 0.02 to 0.07
- obs_loc: int32 [16, 64], P('tile'), may hold values from 0 to 3071
- observed: float32 [2, 16, 64], P(None, 'tile'), may hold values from -6 to 6
- obs_var: float32 [16, 64], P('tile'), may hold values from 0.1 to 1
- ancestors: int32 [2, 16, 256], P(None, 'tile'), may hold values from 0 to 255, as said below
Outputs:
- ensemble: float32 [256, 4, 128, 384], P('dom', None, 'tile')
- averages: float32 [2, 4, 128, 384], P(None, None, 'tile')
Inputs may be any that keep to these rules, and one draw needn't show every extreme that they name: `ancestors`: for every cycle, tile and group of 16 consecutive new particles, at most 2 of them descend from particles of one group of 16 consecutive old particles, and some group of old particles gives exactly 2.
All inputs are finite; a program needn't handle non-finite values.
Results may differ from a plain program's by a relative error of at most 0.0003.
Values sent between devices are 32-bit elements; how exact they have to be, the bound alone decides.
A program may use at most 64 MiB of HBM per device.

v0:
```python
import jax
import jax.numpy as jnp
from jax import lax
from jax.experimental import pallas as pl
from jax.experimental.pallas import tpu as pltpu
from jax.sharding import PartitionSpec as P

MESH = pl.DeviceIdType.MESH
STEPS = 4
CYCLES = 2
FIELDS = 4
PER = 16
GROUPS = 16
CHIPS = 8
ALL = PER * GROUPS
PAIRS = ALL // 2
TILES = 16
ROWS = 8
COLS = 384
LANES = 128
HALF = LANES // 2
NOBS = 64
CHUNKS = 2
PAIR = 2
PARTS = 4
SLOTS = FIELDS + PAIR
STRIPS = 8
WIDE = COLS // STRIPS
EDGE = STEPS
SPAN = WIDE + 2 * EDGE
BLOCKS = 4
BLOCK = PAIRS // BLOCKS


def half_turn(x):
    return pltpu.roll(x, 4, axis=0)


def place(vector, spans, rows=ROWS):
    lane = lax.broadcasted_iota(jnp.int32, (rows, LANES), 1)
    result = None
    for begin, column, length, load, limit in spans:
        low, high = max(begin, vector * LANES), min(begin + length, (vector + 1) * LANES)
        if low >= high:
            continue
        column = column + low - begin
        low, high = low - vector * LANES, high - vector * LANES
        first = max(column, 0) // LANES
        last = min(column + high - low, limit) - 1
        for u in range(first, last // LANES + 1):
            piece = load(u)
            shift = (low - column + LANES * u) % LANES
            if shift:
                piece = pltpu.roll(piece, shift, axis=1)
            start = max(low, low - column + LANES * u)
            result = piece if result is None else jnp.where(lane >= start, piece, result)
    return result


def kernel(members, noise, courant, diffusion, obs_loc, observed, obs_var, ancestors, out, averages,
           out_v, averages_v,
           members_v, noise_v, courant_v, diffusion_v, obs_loc_s, observed_s, obs_var_s, ancestors_s,
           noise_send, noise_recv, late_send, late_recv, late_rows, state_send, state_recv, back_send, back_recv,
           to_north, to_south, from_north, from_south,
           state, result, raw, raw_north, raw_south, coef, obs_weight, obs_mean, obs_rest, partial, weights,
           like_send, like_recv, mean_own,
           noise_pairs, twins, grid2, lone, coef2, windows, obs2, weights2, like_send2, like_recv2,
           mean_send2, mean_recv2,
           sem_load, sem_store, sem_out, sem_in, sem_halo_out, sem_halo_in, sem_halo2_out, sem_halo2_in, sem_raw_out,
           sem_raw_in, sem_small_out, sem_small_in):
    me = lax.axis_index("dom")
    tile = lax.axis_index("tile")
    north = lax.rem(tile + TILES - 1, TILES)
    south = lax.rem(tile + 1, TILES)
    strip = lax.rem(me, STRIPS)
    in_pair = lax.div(me, STRIPS)
    chip = lax.div(me, 2)
    core = lax.rem(me, 2)

    def peer(step):
        return lax.rem(me + step, GROUPS)

    barrier = pltpu.get_barrier_semaphore()

    def greet(step, carry):
        pl.semaphore_signal(barrier, inc=1, device_id={"dom": peer(step)}, device_id_type=MESH)
        return carry

    for neighbour in (north, south):
        pl.semaphore_signal(barrier, inc=1, device_id={"tile": neighbour}, device_id_type=MESH)
    lax.fori_loop(1, GROUPS, greet, 0)

    loads = []

    def load(source, target):
        loads.append(pltpu.make_async_copy(source, target, sem_load.at[len(loads)]))
        loads[-1].start()

    for chunk in range(CHUNKS):
        two = pl.ds(PAIR * chunk, PAIR)
        load(noise.at[1, :, two], noise_v.at[1, :, two])
        load(members.at[:, two], members_v.at[:, two])
        load(noise.at[0, :, two], noise_v.at[0, :, two])
    for source, target in ((courant, courant_v), (diffusion, diffusion_v), (obs_loc, obs_loc_s),
                           (observed, observed_s), (obs_var, obs_var_s), (ancestors, ancestors_s)):
        load(source, target)

    upper = lax.broadcasted_iota(jnp.int32, (ROWS, COLS), 0) < 4
    upper1 = lax.broadcasted_iota(jnp.int32, (ROWS, LANES), 0) < 4
    column = lax.broadcasted_iota(jnp.int32, (ROWS, COLS), 1)
    lane8 = lax.broadcasted_iota(jnp.int32, (ROWS, LANES), 1)
    has_north = jnp.where(tile > 0, 1.0, 0.0).astype(jnp.float32)
    has_south = jnp.where(tile < TILES - 1, 1.0, 0.0).astype(jnp.float32)

    def exchange(source_of, target_of, out_sem, in_sem):
        def one(step, carry):
            near = lax.div(step + 1, 2)
            other = peer(jnp.where(lax.rem(step, 2) == 1, near, GROUPS - near))
            pltpu.make_async_remote_copy(
                src_ref=source_of(other), dst_ref=target_of(me), send_sem=out_sem, recv_sem=in_sem,
                device_id={"dom": other}, device_id_type=MESH,
            ).start()
            return carry

        lax.fori_loop(1, GROUPS, one, 0)

    def await_bytes(ref, sem):
        pltpu.make_async_copy(ref, ref, sem).wait()

    def others(ref, chunk):
        return ref.at[chunk, pl.ds(0, GROUPS - 1)]

    def tile_copy(source, target, out_sem, in_sem, southward):
        return pltpu.make_async_remote_copy(
            src_ref=source, dst_ref=target, send_sem=out_sem, recv_sem=in_sem,
            device_id={"tile": south if southward else north}, device_id_type=MESH,
        )

    def halo_copy(field, southward):
        source, target = (to_south, from_north) if southward else (to_north, from_south)
        way = 1 if southward else 0
        return tile_copy(source.at[field], target.at[field], sem_halo_out.at[field, way], sem_halo_in.at[field, way],
                         southward)

    def halo_copy2(chunk, block, southward):
        source, target = (ROWS, 0) if southward else (EDGE, ROWS + EDGE)
        way = 1 if southward else 0
        rows = EDGE * BLOCK
        return tile_copy(grid2.at[chunk, block, pl.ds(source * BLOCK, rows)],
                         grid2.at[chunk, block, pl.ds(target * BLOCK, rows)], sem_halo2_out.at[chunk, block, way],
                         sem_halo2_in.at[chunk, block, way], southward)

    def raw_copy(part, southward):
        rows = pl.ds(3 * part, 3)
        target = raw_north if southward else raw_south
        way = 1 if southward else 0
        return tile_copy(raw.at[rows], target.at[rows], sem_raw_out.at[part, way], sem_raw_in.at[part, way], southward)

    def begin(field):
        def start_of(particle):
            if field < FIELDS:
                return members_v[particle, field] + noise_v[0, particle, field]
            return noise_v[1, particle, field - PAIR]

        def pair(i, carry):
            first, second = 2 * i, 2 * i + 1
            v0, v1 = start_of(first), start_of(second)
            r0, r1 = half_turn(v0), half_turn(v1)
            state[field, first] = r0
            state[field, second] = r1
            to_south[field, i] = jnp.where(upper, r0, v1)
            to_north[field, i] = jnp.where(upper, v0, r1)
            return carry

        lax.fori_loop(0, PER // 2, pair, 0, unroll=2)

    def forecast(field):
        by = field if field < FIELDS else field - PAIR

        def four(q, carry):
            for i in (2 * q, 2 * q + 1):
                top = from_north[field, i] * has_north
                bottom = from_south[field, i] * has_south
                for k, (above, below) in enumerate(((top, half_turn(bottom)), (half_turn(top), bottom))):
                    particle = 2 * i + k
                    r = state[field, particle]
                    x = jnp.concatenate([jnp.where(upper, above, r), jnp.where(upper, r, below)], axis=0)
                    for _ in range(STEPS):
                        x = (coef[by, 0] * x + coef[by, 1] * pltpu.roll(x, 1, axis=0)
                             + coef[by, 2] * pltpu.roll(x, 2 * ROWS - 1, axis=0)
                             + coef[by, 3] * pltpu.roll(x, 1, axis=1)
                             + coef[by, 4] * pltpu.roll(x, COLS - 1, axis=1))
                    v = half_turn(jnp.where(upper, x[ROWS:], x[:ROWS]))
                    result[field, particle] = v
                    if field == 0:
                        miss = v - obs_mean[0]
                        cost = obs_weight[...] * miss * miss + obs_rest[0]
                        cost = cost[:, :LANES] + cost[:, LANES:2 * LANES] + cost[:, 2 * LANES:]
                        partial[pl.ds(particle, 1), :] = jnp.sum(cost, axis=0, keepdims=True)
            return carry

        lax.fori_loop(0, PER // 4, four, 0)

    def pack(chunk, get, outgoing, incoming):
        def one(f, carry):
            for g in range(STRIPS):
                def loader(k):
                    return lambda u: get(k, PAIR * chunk + f, pl.ds(LANES * u, LANES))

                spans = [(SPAN * k, WIDE * g - EDGE, SPAN, loader(k), COLS) for k in range(PER)]
                for j in range(PER * SPAN // LANES):
                    outgoing[chunk, STRIPS * f + g, :, LANES * j:LANES * (j + 1)] = place(j, spans)
            return carry

        lax.fori_loop(0, PAIR, one, 0)
        incoming[chunk, me] = outgoing[chunk, me]

    def swap(outgoing, incoming, chunk, which):
        exchange(lambda other: outgoing.at[chunk, other], lambda mine: incoming.at[chunk, mine],
                 sem_out.at[chunk, which], sem_in.at[chunk, which])

    def pack_late():
        def one(f, carry):
            for g in range(STRIPS):
                def loader(k):
                    return lambda u: result[FIELDS + f, k, :, pl.ds(LANES * u, LANES)]

                spans = [(WIDE * k, WIDE * g, WIDE, loader(k), COLS) for k in range(PER)]
                for j in range(PER * WIDE // LANES):
                    late_send[STRIPS * f + g, :, LANES * j:LANES * (j + 1)] = place(j, spans)
            return carry

        lax.fori_loop(0, PAIR, one, 0)
        late_recv[me] = late_send[me]

    def swap_late():
        exchange(lambda other: late_send.at[other], lambda mine: late_recv.at[mine], sem_out.at[1, 0], sem_in.at[1, 0])

    def add_late():
        await_bytes(late_recv.at[pl.ds(0, GROUPS - 1)], sem_in.at[1, 0])

        def one(s, carry):
            def load_from(u):
                return late_recv[s, :, LANES * u:LANES * (u + 1)]

            for m in range(PER // 2):
                late_rows[pl.ds(PER // 2 * s + m, ROWS, stride=PAIRS), :] = place(
                    0, [(HALF * h + EDGE, WIDE * (2 * m + h), WIDE, load_from, PER * WIDE) for h in range(2)])
            return carry

        lax.fori_loop(0, GROUPS, one, 0, unroll=4)

    def sum_late():
        for r in range(ROWS):
            x = lone[1, ALL * r:ALL * r + PAIRS, :] + late_rows[PAIRS * r:PAIRS * (r + 1), :]
            lone[1, ALL * r:ALL * r + PAIRS, :] = x
            lone[1, ALL * r + PAIRS:ALL * (r + 1), :] = pltpu.roll(x, HALF, axis=1)

    def unpack_noise(chunk):
        await_bytes(others(noise_recv, chunk), sem_in.at[chunk, 0])

        def one(s, carry):
            def load_from(u):
                return noise_recv[chunk, s, :, LANES * u:LANES * (u + 1)]

            for m in range(PER // 2):
                noise_pairs[chunk, PER // 2 * s + m] = place(
                    0, [(HALF * h, SPAN * (2 * m + h), SPAN, load_from, PER * SPAN) for h in range(2)])
            return carry

        lax.fori_loop(0, GROUPS, one, 0, unroll=4)

    def unpack_state(chunk):

        def one(s, carry):
            def load_from(u):
                return state_recv[chunk, s, :, LANES * u:LANES * (u + 1)]

            for k in range(PER):
                twins[chunk, PER * s + k] = place(
                    0, [(HALF * h, SPAN * k, SPAN, load_from, PER * SPAN) for h in range(2)])
            return carry

        lax.fori_loop(0, GROUPS, one, 0, unroll=2)

    def begin2(chunk, block):
        left = lane8 < HALF

        def one(i, carry):
            m = BLOCK * block + i
            old0, old1 = ancestors_s[0, 0, 2 * m], ancestors_s[0, 0, 2 * m + 1]
            v = jnp.where(left, twins[chunk, old0], twins[chunk, old1])
            if chunk == 0:
                v = v + noise_pairs[chunk, m]
            grid2[chunk, block, pl.ds(EDGE * BLOCK + i, ROWS, stride=BLOCK), :] = v
            return carry

        lax.fori_loop(0, BLOCK, one, 0, unroll=8)
        halo_copy2(chunk, block, True).start()
        halo_copy2(chunk, block, False).start()

    def forecast2(chunk, block):
        halo_copy2(chunk, block, True).wait_recv()
        halo_copy2(chunk, block, False).wait_recv()
        high = ROWS + 2 * EDGE

        def tall(n, r):
            return jnp.concatenate([coef2[chunk, n, r]] * (BLOCK // ROWS), axis=0)

        x = [grid2[chunk, block, BLOCK * r:BLOCK * (r + 1), :] for r in range(high)]
        x = [v * has_north if r < EDGE else v * has_south if r >= EDGE + ROWS else v for r, v in enumerate(x)]
        for s in range(1, STEPS + 1):
            new = list(x)
            for r in range(s, high - s):
                new[r] = (tall(0, r) * x[r] + tall(1, r) * x[r - 1] + tall(2, r) * x[r + 1]
                          + tall(3, r) * pltpu.roll(x[r], 1, axis=1) + tall(4, r) * pltpu.roll(x[r], LANES - 1, axis=1))
            x = new
        for r in range(ROWS):
            lone[chunk, ALL * r + BLOCK * block:ALL * r + BLOCK * (block + 1), :] = x[EDGE + r]
            if chunk == 0:
                low = ALL * r + PAIRS + BLOCK * block
                lone[chunk, low:low + BLOCK, :] = pltpu.roll(x[EDGE + r], HALF, axis=1)

    def pack_back(chunk):
        def one(group, carry):
            def loader(j):
                old = ancestors_s[1, 0, PER * group + j]
                tall = lone[chunk, pl.ds((old & 1) * PAIRS + (old >> 1), ROWS, stride=ALL), :]
                return lambda u: tall

            spans = [(WIDE * j, EDGE, WIDE, loader(j), LANES) for j in range(PER)]
            for n in range(PER * WIDE // LANES):
                back_send[chunk, group, :, LANES * n:LANES * (n + 1)] = place(n, spans)
            return carry

        lax.fori_loop(0, GROUPS, one, 0, unroll=4)
        back_recv[chunk, me] = back_send[chunk, me]

    def stores(chunk):
        two = pl.ds(PAIR * chunk, PAIR)
        return (pltpu.make_async_copy(out_v.at[:, two], out.at[:, two], sem_store.at[chunk, 0]),
                pltpu.make_async_copy(averages_v.at[:, two], averages.at[:, two], sem_store.at[chunk, 1]))

    def finish(chunk):
        await_bytes(others(back_recv, chunk), sem_in.at[chunk, 2])

        def one(f, carry):
            def loader(g):
                return lambda u: back_recv[chunk, STRIPS * f + g, :, LANES * u:LANES * (u + 1)]

            for j in range(PER):
                spans = [(WIDE * g, WIDE * j, WIDE, loader(g), PER * WIDE) for g in range(STRIPS)]
                for u in range(COLS // LANES):
                    out_v[j, PAIR * chunk + f, :, LANES * u:LANES * (u + 1)] = place(u, spans)
            return carry

        lax.fori_loop(0, PAIR, one, 0)

    lane = lax.broadcasted_iota(jnp.int32, (PER, LANES), 1)
    line = lax.broadcasted_iota(jnp.int32, (PER, LANES), 0)

    def likelihood():
        total = -0.5 * jnp.sum(partial[...], axis=1, keepdims=True)
        row = jnp.sum(jnp.where(lane == line, total, 0.0), axis=0, keepdims=True)
        like_send[...] = row
        like_recv[me] = row
        exchange(lambda other: like_send, lambda mine: like_recv.at[mine], sem_small_out.at[0], sem_small_in.at[0])

    def weigh():
        await_bytes(like_recv.at[pl.ds(0, GROUPS - 1)], sem_small_in.at[0])
        everyone = like_recv[...]
        known = lax.broadcasted_iota(jnp.int32, (GROUPS, 1, LANES), 2) < PER
        peak = jnp.max(jnp.where(known, everyone, -3.0e38), axis=0)
        peak = jnp.max(peak, axis=1, keepdims=True)
        shifted = jnp.where(known, jnp.exp(jnp.where(known, everyone - peak[None], 0.0)), 0.0)
        total = jnp.sum(jnp.sum(shifted, axis=0), axis=1, keepdims=True)
        weight = shifted / total[None]
        for g in range(GROUPS):
            own = jnp.sum(jnp.where(lane == line, weight[g], 0.0), axis=1, keepdims=True)
            weights[PER * g:PER * (g + 1), :] = jnp.broadcast_to(own, (PER, LANES))

    def average(chunk):
        def add(q, sums):
            return tuple(s + weights[pl.ds(4 * q + k, 1), :] * twins[chunk, 4 * q + k] for k, s in enumerate(sums))

        sums = lax.fori_loop(0, ALL // 4, add, (jnp.zeros((ROWS, LANES), jnp.float32),) * 4, unroll=4)
        mean_own[chunk] = (sums[0] + sums[1]) + (sums[2] + sums[3])

    place2 = lax.broadcasted_iota(jnp.int32, (PAIRS, LANES), 1)
    line2 = lax.broadcasted_iota(jnp.int32, (PAIRS, LANES), 0)

    def likelihood2():
        cost = jnp.zeros((PAIRS, LANES), jnp.float32)
        for r in range(ROWS):
            miss = lone[0, ALL * r:ALL * r + PAIRS, :] - obs2[1, r:r + 1]
            cost = cost + obs2[0, r:r + 1] * miss * miss + obs2[2, r:r + 1]
        for h in range(2):
            side = (place2 < HALF) if h == 0 else (place2 >= HALF)
            total = -0.5 * jnp.sum(jnp.where(side, cost, 0.0), axis=1, keepdims=True)
            row = jnp.sum(jnp.where(place2 == line2, total, 0.0), axis=0, keepdims=True)
            like_send2[h:h + 1, :] = row
        like_recv2[me] = like_send2[...]
        exchange(lambda other: like_send2, lambda mine: like_recv2.at[mine], sem_small_out.at[1], sem_small_in.at[1])

    def weigh2():
        await_bytes(like_recv2.at[pl.ds(0, GROUPS - 1)], sem_small_in.at[1])
        total = like_recv2[0]
        for g in range(1, GROUPS):
            total = total + like_recv2[g]
        peak = jnp.max(jnp.max(total, axis=0, keepdims=True), axis=1, keepdims=True)
        shifted = jnp.exp(total - peak)
        weight = shifted / jnp.sum(jnp.sum(shifted, axis=0, keepdims=True), axis=1, keepdims=True)
        sides = [jnp.sum(jnp.where(place2 == line2, weight[h:h + 1], 0.0), axis=1, keepdims=True) for h in range(2)]
        weights2[...] = jnp.where(place2 < HALF, sides[0], sides[1])

    def average2(chunk):
        for r in range(ROWS):
            part = weights2[...] * lone[chunk, ALL * r:ALL * r + PAIRS, :]
            mean_send2[chunk, r:r + 1, :] = jnp.sum(part, axis=0, keepdims=True)
        total = mean_send2[chunk]
        total = total + pltpu.roll(total, HALF, axis=1)
        total = jnp.where(lane8 < HALF, mean_own[chunk], total)
        mean_send2[chunk] = total
        mean_recv2[chunk, core, chip] = total

        def one(step, carry):
            pltpu.make_async_remote_copy(
                src_ref=mean_send2.at[chunk], dst_ref=mean_recv2.at[chunk, core, chip],
                send_sem=sem_small_out.at[2 + chunk], recv_sem=sem_small_in.at[2 + chunk],
                device_id={"dom": 2 * lax.rem(chip + step, CHIPS) + core}, device_id_type=MESH,
            ).start()
            return carry

        lax.fori_loop(1, CHIPS, one, 0)

    def means_across(chunk):
        return pltpu.make_async_remote_copy(
            src_ref=mean_recv2.at[chunk, core], dst_ref=mean_recv2.at[chunk, core],
            send_sem=sem_small_out.at[4 + chunk], recv_sem=sem_small_in.at[4 + chunk],
            device_id={"dom": 2 * chip + 1 - core}, device_id_type=MESH,
        )

    def pass_means(chunk):
        await_bytes(mean_recv2.at[chunk, 0, pl.ds(0, CHIPS - 1)], sem_small_in.at[2 + chunk])
        means_across(chunk).start()

    def write_means(chunk):
        means_across(chunk).wait_recv()
        for c in range(CYCLES):
            for f in range(PAIR):
                def loader(g):
                    return lambda u: mean_recv2[chunk, g % 2, (STRIPS * f + g) // 2]

                spans = [(WIDE * g, HALF * c + EDGE, WIDE, loader(g), LANES) for g in range(STRIPS)]
                for u in range(COLS // LANES):
                    averages_v[c, PAIR * chunk + f, :, LANES * u:LANES * (u + 1)] = place(u, spans)

    def edge_coefficients():
        for m in range(2):
            raw[m] = half_turn(courant_v[m])
        for f in range(FIELDS):
            raw[2 + f] = half_turn(diffusion_v[f])

    def coefficients(field):
        def sixteen(m):
            mid = raw[m]
            return jnp.concatenate([jnp.where(upper, raw_north[m], mid), jnp.where(upper, mid, raw_south[m])], axis=0)

        inside = jnp.concatenate([jnp.where(upper, has_north, 1.0), jnp.where(upper, 1.0, has_south)], axis=0)
        column2 = jnp.concatenate([column, column], axis=0)
        cx, cy, d = sixteen(0), sixteen(1), sixteen(2 + field)
        coef[field, 0] = inside * (1.0 - jnp.abs(cx) - jnp.abs(cy) - 4.0 * d)
        coef[field, 1] = inside * (jnp.maximum(cx, 0.0) + d)
        coef[field, 2] = inside * (d - jnp.minimum(cx, 0.0))
        coef[field, 3] = jnp.where(column2 > 0, inside * (jnp.maximum(cy, 0.0) + d), 0.0)
        coef[field, 4] = jnp.where(column2 < COLS - 1, inside * (d - jnp.minimum(cy, 0.0)), 0.0)

    def window(get, rows):
        for g in range(STRIPS):
            spans = [(HALF * h, WIDE * g - EDGE, SPAN, lambda u: get(pl.ds(LANES * u, LANES)), COLS) for h in range(2)]
            windows[g, :rows] = place(0, spans, rows)
        return windows[strip, :rows]

    def coefficients2(chunk):
        lane16 = lax.broadcasted_iota(jnp.int32, (2 * ROWS, LANES), 1)
        used = lax.rem(lane16, HALF) < SPAN
        for n in range(5):
            here = window(lambda cols: coef[PAIR * chunk + in_pair, n, :, cols], 2 * ROWS)
            here = jnp.where(used, here, 0.0)
            for r in range(2 * ROWS):
                coef2[chunk, n, r] = jnp.broadcast_to(here[r:r + 1], (ROWS, LANES))

    def observations():
        cell = lax.broadcasted_iota(jnp.int32, (ROWS, COLS), 0) * COLS + column
        zero = jnp.zeros((ROWS, COLS), jnp.float32)

        def gather(k, sums):
            here = cell == obs_loc_s[0, k]
            precision = jnp.where(here, 1.0 / jnp.full((1, COLS), obs_var_s[0, k], jnp.float32), 0.0)
            return (sums[0] + precision,) + tuple(sums[1 + c] + precision * observed_s[c, 0, k] for c in range(CYCLES))

        sums = lax.fori_loop(0, NOBS, gather, (zero,) * (1 + CYCLES), unroll=8)
        obs_weight[...] = sums[0]
        seen = sums[0] > 0.0
        means = []
        for c in range(CYCLES):
            means.append(jnp.where(seen, sums[1 + c] / jnp.where(seen, sums[0], 1.0), 0.0))
            obs_mean[c] = means[c]

        def rest(k, sums):
            here = cell == obs_loc_s[0, k]
            precision = jnp.where(here, 1.0 / jnp.full((1, COLS), obs_var_s[0, k], jnp.float32), 0.0)
            return tuple(sums[c] + precision * (observed_s[c, 0, k] - means[c]) * (observed_s[c, 0, k] - means[c])
                         for c in range(CYCLES))

        sums = lax.fori_loop(0, NOBS, rest, (zero,) * CYCLES, unroll=8)
        for c in range(CYCLES):
            obs_rest[c] = sums[c]

    def observations2():
        inner = lax.rem(lane8, HALF)
        own = (inner >= EDGE) & (inner < EDGE + WIDE)
        first = jnp.where(in_pair == 0, 1.0, 0.0).astype(jnp.float32)
        obs2[0] = jnp.where(own, window(lambda cols: obs_weight[:, cols], ROWS), 0.0) * first
        obs2[1] = window(lambda cols: obs_mean[1, :, cols], ROWS)
        obs2[2] = jnp.where(own, window(lambda cols: obs_rest[1, :, cols], ROWS), 0.0) * first

    def noise_of(k, field, cols):
        return noise_v[1, k, field, :, cols]

    def state_of(k, field, cols):
        return result[field, k, :, cols]

    loads[0].wait()
    pack(0, noise_of, noise_send, noise_recv)
    for n in (1, 2, 6, 7):
        loads[n].wait()
    edge_coefficients()
    begin(0)
    pl.semaphore_wait(barrier, GROUPS + 1)

    def edges(ready):
        for way in (True, False):
            halo_copy(ready, way).wait_recv()

    def send_edges(field):
        for way in (True, False):
            halo_copy(field, way).start()

    for way in (True, False):
        raw_copy(0, way).start()
    send_edges(0)
    swap(noise_send, noise_recv, 0, 0)
    begin(1)
    send_edges(1)
    for way in (True, False):
        raw_copy(1, way).start()
    for n in (3, 4, 5, 8, 9, 10, 11):
        loads[n].wait()
    for f in range(2, FIELDS):
        begin(f)
    observations()
    for way in (True, False):
        raw_copy(0, way).wait_recv()
    coefficients(0)
    edges(0)
    send_edges(2)
    forecast(0)
    likelihood()
    for way in (True, False):
        raw_copy(1, way).wait_recv()
    coefficients(1)
    edges(1)
    send_edges(3)
    forecast(1)
    pack(0, state_of, state_send, state_recv)
    swap(state_send, state_recv, 0, 1)
    for f in range(2, FIELDS):
        coefficients(f)
        edges(f)
        begin(f + PAIR)
        send_edges(f + PAIR)
        forecast(f)
    pack(1, state_of, state_send, state_recv)
    swap(state_send, state_recv, 1, 1)
    for chunk in range(CHUNKS):
        coefficients2(chunk)
    observations2()
    unpack_noise(0)
    for f in range(FIELDS, SLOTS):
        edges(f)
        forecast(f)
    pack_late()
    swap_late()
    weigh()
    await_bytes(others(state_recv, 0), sem_in.at[0, 1])
    unpack_state(0)
    for block in range(BLOCKS):
        begin2(0, block)
    average(0)
    for block in range(BLOCKS):
        forecast2(0, block)
    likelihood2()
    pack_back(0)
    swap(back_send, back_recv, 0, 2)
    await_bytes(others(state_recv, 1), sem_in.at[1, 1])
    unpack_state(1)
    for block in range(BLOCKS):
        begin2(1, block)
    weigh2()
    average2(0)
    average(1)
    for block in range(BLOCKS):
        forecast2(1, block)
    add_late()
    sum_late()
    average2(1)
    pack_back(1)
    swap(back_send, back_recv, 1, 2)
    pass_means(0)
    finish(0)
    write_means(0)
    for copy in stores(0):
        copy.start()
    pass_means(1)
    finish(1)
    stores(1)[0].start()
    write_means(1)
    stores(1)[1].start()
    await_bytes(others(noise_recv, 0), sem_out.at[0, 0])
    await_bytes(late_recv.at[pl.ds(0, GROUPS - 1)], sem_out.at[1, 0])
    for chunk in range(CHUNKS):
        await_bytes(others(state_recv, chunk), sem_out.at[chunk, 1])
    for chunk in range(CHUNKS):
        await_bytes(others(back_recv, chunk), sem_out.at[chunk, 2])
        await_bytes(mean_recv2.at[chunk, 0, pl.ds(0, CHIPS - 1)], sem_small_out.at[2 + chunk])
        means_across(chunk).wait_send()
        for copy in stores(chunk):
            copy.wait()
    for way in (True, False):
        for f in range(SLOTS):
            halo_copy(f, way).wait_send()
        for part in range(2):
            raw_copy(part, way).wait_send()
        for chunk in range(CHUNKS):
            for block in range(BLOCKS):
                halo_copy2(chunk, block, way).wait_send()
    for n, ref in enumerate((like_recv, like_recv2)):
        await_bytes(ref.at[pl.ds(0, GROUPS - 1)], sem_small_out.at[n])


def hand_over(ensemble, averages, ensemble_out, averages_out, ensemble_v, averages_v, sem_in, sem_out):
    size = PER // PARTS
    ways = [(ensemble.at[pl.ds(size * n, size)], ensemble_v.at[pl.ds(size * n, size)],
             ensemble_out.at[pl.ds(size * n, size)]) for n in range(PARTS)]
    ways.append((averages, averages_v, averages_out))
    into = [pltpu.make_async_copy(source, middle, sem_in.at[n]) for n, (source, middle, _) in enumerate(ways)]
    away = [pltpu.make_async_copy(middle, target, sem_out.at[n]) for n, (_, middle, target) in enumerate(ways)]
    for copy in into:
        copy.start()
    for first, second in zip(into, away):
        first.wait()
        second.start()
    for copy in away:
        copy.wait()


def per_device(members, noise, courant, diffusion, obs_loc, observed, obs_var, ancestors):
    f32 = jnp.float32
    anywhere = pl.BlockSpec(memory_space=pl.ANY)
    plane = (ROWS, COLS)
    one = (ROWS, LANES)
    operands = (members, noise, courant, diffusion, obs_loc, observed, obs_var, ancestors)

    def vmem(*shape):
        return pltpu.VMEM(shape, f32)

    scratch = [vmem(PER, FIELDS, *plane), vmem(CYCLES, FIELDS, *plane)]
    scratch += [vmem(*a.shape) for a in operands[:4]] + [pltpu.SMEM(a.shape, a.dtype) for a in operands[4:]]
    scratch += [vmem(1, GROUPS, ROWS, PER * SPAN) for _ in range(2)]
    scratch += [vmem(GROUPS, ROWS, PER * WIDE) for _ in range(2)] + [vmem(ROWS * PAIRS, LANES)]
    scratch += [vmem(CHUNKS, GROUPS, ROWS, PER * SPAN) for _ in range(2)]
    scratch += [vmem(CHUNKS, GROUPS, ROWS, PER * WIDE) for _ in range(2)]
    scratch += [vmem(SLOTS, PER // 2, *plane) for _ in range(4)]
    scratch += [
        vmem(SLOTS, PER, *plane),
        vmem(SLOTS, PER, *plane),
        vmem(2 + FIELDS, *plane),
        vmem(2 + FIELDS, *plane),
        vmem(2 + FIELDS, *plane),
        vmem(FIELDS, 5, 2 * ROWS, COLS),
        vmem(*plane),
        vmem(CYCLES, *plane),
        vmem(CYCLES, *plane),
        vmem(PER, LANES),
        vmem(ALL, LANES),
        vmem(1, LANES),
        vmem(GROUPS, 1, LANES),
        vmem(CHUNKS, *one),
        vmem(1, PAIRS, *one),
        vmem(CHUNKS, ALL, *one),
        vmem(CHUNKS, BLOCKS, (ROWS + 2 * EDGE) * BLOCK, LANES),
        vmem(CHUNKS, ROWS * ALL, LANES),
        vmem(CHUNKS, 5, 2 * ROWS, *one),
        vmem(STRIPS, 2 * ROWS, LANES),
        vmem(3, *one),
        vmem(PAIRS, LANES),
        vmem(2, LANES),
        vmem(GROUPS, 2, LANES),
        vmem(CHUNKS, *one),
        vmem(CHUNKS, 2, CHIPS, *one),
        pltpu.SemaphoreType.DMA((12,)),
        pltpu.SemaphoreType.DMA((CHUNKS, 2)),
        pltpu.SemaphoreType.DMA((CHUNKS, 3)),
        pltpu.SemaphoreType.DMA((CHUNKS, 3)),
        pltpu.SemaphoreType.DMA((SLOTS, 2)),
        pltpu.SemaphoreType.DMA((SLOTS, 2)),
        pltpu.SemaphoreType.DMA((CHUNKS, BLOCKS, 2)),
        pltpu.SemaphoreType.DMA((CHUNKS, BLOCKS, 2)),
        pltpu.SemaphoreType.DMA((2, 2)),
        pltpu.SemaphoreType.DMA((2, 2)),
        pltpu.SemaphoreType.DMA((6,)),
        pltpu.SemaphoreType.DMA((6,)),
    ]
    results = pl.pallas_call(
        kernel,
        out_shape=(
            jax.ShapeDtypeStruct((PER, FIELDS) + plane, f32),
            jax.ShapeDtypeStruct((CYCLES, FIELDS) + plane, f32),
        ),
        in_specs=[anywhere] * 8,
        out_specs=(anywhere, anywhere),
        scratch_shapes=scratch,
        compiler_params=pltpu.CompilerParams(
            collective_id=0, has_side_effects=True, vmem_limit_bytes=60 * 1024 * 1024
        ),
        name="assimilate",
    )(*operands)
    return pl.pallas_call(
        hand_over,
        out_shape=tuple(jax.ShapeDtypeStruct(r.shape, f32) for r in results),
        in_specs=[anywhere] * 2,
        out_specs=(anywhere, anywhere),
        scratch_shapes=[vmem(*r.shape) for r in results] + [pltpu.SemaphoreType.DMA((PARTS + 1,))] * 2,
        compiler_params=pltpu.CompilerParams(vmem_limit_bytes=60 * 1024 * 1024),
        name="hand_over",
    )(*results)


def solution(mesh):
    return jax.shard_map(
        per_device,
        mesh=mesh,
        in_specs=(
            P("dom", None, "tile", None),
            P(None, "dom", None, "tile", None),
            P(None, "tile", None),
            P(None, "tile", None),
            P("tile", None),
            P(None, "tile", None),
            P("tile", None),
            P(None, "tile", None),
        ),
        out_specs=(P("dom", None, "tile", None), P(None, None, "tile", None)),
        check_vma=False,
    )
```

profile of v0, /device:TPU:1, one launch (start us, length us, event | category | flops | bytes accessed | tf_op | source)
XLA Modules:
  0.0 77.6 jit_solution(3034212931897772633)
XLA Ops:
  0.6 74.9 %assimilate.1 = (f32[16,4,8,384]{3,2,1,0:T(8,128)}, f32[2,4,8,384]{3,2,1,0:T(8,128)}) custom-call(f32[16,4,8,384]{3,2,1,0:T(8,128)} %members.1, f32[2,16,4,8,384]{4,3,2,1,0:T(8,128)} %noise.1, f32[2,8,384]{2,1,0:T(8,128)} %courant.1, f32[4,8,384]{2,1,0:T(8,128)} %diffusion.1, s32[1,64]{1,0:T(1,128)} %obs_loc.1, f32[2,1,64]{2,1,0:T(1,128)} %observed.1, ...), custom_call_target="tpu_custom_call" | custom-call | tf_op jit(solution)/shard_map/assimilate/pallas_call | solution.py:725
  75.6 2.0 %hand_over.1 = (f32[16,4,8,384]{3,2,1,0:T(8,128)}, f32[2,4,8,384]{3,2,1,0:T(8,128)}) custom-call(f32[16,4,8,384]{3,2,1,0:T(8,128)} %get-tuple-element.4.ensemble, f32[2,4,8,384]{3,2,1,0:T(8,128)} %get-tuple-element.5.averages), custom_call_target="tpu_custom_call" | custom-call | tf_op jit(solution)/shard_map/hand_over/pallas_call | solution.py:739
where the time goes:
time: 77.7 us; the launch traced here: 77.6 us
  Pallas kernels  76.9 us (99%)
    pallas_call x1, Pallas kernels, per_device(): pl.pallas_call(kernel, out_shape=(jax.ShapeDtypeStruct((PER, FIELDS) + pl...  74.9 us
    pallas_call x1, Pallas kernels, per_device(): pl.pallas_call(hand_over, out_shape=tuple((jax.ShapeDtypeStruct(r.shape,...  2.01 us

commit v1 on v0

--- a/solution.py
+++ b/solution.py
@@ -678,7 +678,7 @@
     scratch = [vmem(PER, FIELDS, *plane), vmem(CYCLES, FIELDS, *plane)]
     scratch += [vmem(*a.shape) for a in operands[:4]] + [pltpu.SMEM(a.shape, a.dtype) for a in operands[4:]]
     scratch += [vmem(1, GROUPS, ROWS, PER * SPAN) for _ in range(2)]
-    scratch += [vmem(GROUPS, ROWS, PER * WIDE) for _ in range(2)] + [vmem(ROWS * PAIRS, LANES)]
+    scratch += [vmem(GROUPS, ROWS, PER * WIDE) for _ in range(2)] + [vmem((ROWS + 1) * PAIRS, LANES)]
     scratch += [vmem(CHUNKS, GROUPS, ROWS, PER * SPAN) for _ in range(2)]
     scratch += [vmem(CHUNKS, GROUPS, ROWS, PER * WIDE) for _ in range(2)]
     scratch += [vmem(SLOTS, PER // 2, *plane) for _ in range(4)]
@@ -700,7 +700,7 @@
         vmem(1, PAIRS, *one),
         vmem(CHUNKS, ALL, *one),
         vmem(CHUNKS, BLOCKS, (ROWS + 2 * EDGE) * BLOCK, LANES),
-        vmem(CHUNKS, ROWS * ALL, LANES),
+        vmem(CHUNKS, (ROWS + 1) * ALL, LANES),
         vmem(CHUNKS, 5, 2 * ROWS, *one),
         vmem(STRIPS, 2 * ROWS, LANES),
         vmem(3, *one),

time: 77.7 us -> 77.7 us (level)
  no operation moved by 1% of the time
where the time goes in v1:
time: 77.7 us; the launch traced here: 77.6 us
  Pallas kernels  76.9 us (99%)
    pallas_call x1, Pallas kernels, per_device(): pl.pallas_call(kernel, out_shape=(jax.ShapeDtypeStruct((PER, FIELDS) + pl...  74.9 us
    pallas_call x1, Pallas kernels, per_device(): pl.pallas_call(hand_over, out_shape=tuple((jax.ShapeDtypeStruct(r.shape,...  2.01 us

profile of v1, /device:TPU:1, one launch (start us, length us, event | category | flops | bytes accessed | tf_op | source)
XLA Modules:
  0.0 77.6 jit_solution(12535089417769676521)
XLA Ops:
  0.6 74.9 %assimilate.1 = (f32[16,4,8,384]{3,2,1,0:T(8,128)}, f32[2,4,8,384]{3,2,1,0:T(8,128)}) custom-call(f32[16,4,8,384]{3,2,1,0:T(8,128)} %members.1, f32[2,16,4,8,384]{4,3,2,1,0:T(8,128)} %noise.1, f32[2,8,384]{2,1,0:T(8,128)} %courant.1, f32[4,8,384]{2,1,0:T(8,128)} %diffusion.1, s32[1,64]{1,0:T(1,128)} %obs_loc.1, f32[2,1,64]{2,1,0:T(1,128)} %observed.1, ...), custom_call_target="tpu_custom_call" | custom-call | tf_op jit(solution)/shard_map/assimilate/pallas_call | solution.py:725
  75.6 2.0 %hand_over.1 = (f32[16,4,8,384]{3,2,1,0:T(8,128)}, f32[2,4,8,384]{3,2,1,0:T(8,128)}) custom-call(f32[16,4,8,384]{3,2,1,0:T(8,128)} %get-tuple-element.4.ensemble, f32[2,4,8,384]{3,2,1,0:T(8,128)} %get-tuple-element.5.averages), custom_call_target="tpu_custom_call" | custom-call | tf_op jit(solution)/shard_map/hand_over/pallas_call | solution.py:739

commit v2 on v1

--- a/solution.py
+++ b/solution.py
@@ -22,7 +22,6 @@
 NOBS = 64
 CHUNKS = 2
 PAIR = 2
-PARTS = 4
 SLOTS = FIELDS + PAIR
 STRIPS = 8
 WIDE = COLS // STRIPS
@@ -57,7 +56,7 @@
     return result
 
 
-def kernel(members, noise, courant, diffusion, obs_loc, observed, obs_var, ancestors, out, averages,
+def kernel(members, noise, courant, diffusion, obs_loc, observed, obs_var, ancestors, out, last, averages,
            out_v, averages_v,
            members_v, noise_v, courant_v, diffusion_v, obs_loc_s, observed_s, obs_var_s, ancestors_s,
            noise_send, noise_recv, late_send, late_recv, late_rows, state_send, state_recv, back_send, back_recv,
@@ -66,7 +65,7 @@
            like_send, like_recv, mean_own,
            noise_pairs, twins, grid2, lone, coef2, windows, obs2, weights2, like_send2, like_recv2,
            mean_send2, mean_recv2,
-           sem_load, sem_store, sem_out, sem_in, sem_halo_out, sem_halo_in, sem_halo2_out, sem_halo2_in, sem_raw_out,
+           sem_load, sem_store, sem_own, sem_out, sem_in, sem_halo_out, sem_halo_in, sem_halo2_out, sem_halo2_in, sem_raw_out,
            sem_raw_in, sem_small_out, sem_small_in):
     me = lax.axis_index("dom")
     tile = lax.axis_index("tile")
@@ -334,12 +333,23 @@
             return carry
 
         lax.fori_loop(0, GROUPS, one, 0, unroll=4)
-        back_recv[chunk, me] = back_send[chunk, me]
+        if chunk == 0:
+            back_recv[chunk, me] = back_send[chunk, me]
+        else:
+            own_back().start()
+
+    def own_back():
+        return pltpu.make_async_copy(back_send.at[1, me], last.at[me], sem_own)
+
+    def swap_last():
+        exchange(lambda other: back_send.at[1, other], lambda mine: last.at[mine], sem_out.at[1, 2], sem_in.at[1, 2])
 
     def stores(chunk):
         two = pl.ds(PAIR * chunk, PAIR)
-        return (pltpu.make_async_copy(out_v.at[:, two], out.at[:, two], sem_store.at[chunk, 0]),
-                pltpu.make_async_copy(averages_v.at[:, two], averages.at[:, two], sem_store.at[chunk, 1]))
+        copies = [pltpu.make_async_copy(averages_v.at[:, two], averages.at[:, two], sem_store.at[chunk, 1])]
+        if chunk == 0:
+            copies.append(pltpu.make_async_copy(out_v, out, sem_store.at[chunk, 0]))
+        return copies
 
     def finish(chunk):
         await_bytes(others(back_recv, chunk), sem_in.at[chunk, 2])
@@ -351,7 +361,7 @@
             for j in range(PER):
                 spans = [(WIDE * g, WIDE * j, WIDE, loader(g), PER * WIDE) for g in range(STRIPS)]
                 for u in range(COLS // LANES):
-                    out_v[j, PAIR * chunk + f, :, LANES * u:LANES * (u + 1)] = place(u, spans)
+                    out_v[j, f, :, LANES * u:LANES * (u + 1)] = place(u, spans)
             return carry
 
         lax.fori_loop(0, PAIR, one, 0)
@@ -616,23 +626,23 @@
     sum_late()
     average2(1)
     pack_back(1)
-    swap(back_send, back_recv, 1, 2)
+    swap_last()
     pass_means(0)
     finish(0)
     write_means(0)
     for copy in stores(0):
         copy.start()
     pass_means(1)
-    finish(1)
+    write_means(1)
     stores(1)[0].start()
-    write_means(1)
-    stores(1)[1].start()
+    await_bytes(last.at[pl.ds(0, GROUPS - 1)], sem_in.at[1, 2])
+    own_back().wait()
     await_bytes(others(noise_recv, 0), sem_out.at[0, 0])
     await_bytes(late_recv.at[pl.ds(0, GROUPS - 1)], sem_out.at[1, 0])
     for chunk in range(CHUNKS):
         await_bytes(others(state_recv, chunk), sem_out.at[chunk, 1])
     for chunk in range(CHUNKS):
-        await_bytes(others(back_recv, chunk), sem_out.at[chunk, 2])
+        await_bytes(others(back_send, chunk), sem_out.at[chunk, 2])
         await_bytes(mean_recv2.at[chunk, 0, pl.ds(0, CHIPS - 1)], sem_small_out.at[2 + chunk])
         means_across(chunk).wait_send()
         for copy in stores(chunk):
@@ -649,18 +659,32 @@
         await_bytes(ref.at[pl.ds(0, GROUPS - 1)], sem_small_out.at[n])
 
 
-def hand_over(ensemble, averages, ensemble_out, averages_out, ensemble_v, averages_v, sem_in, sem_out):
-    size = PER // PARTS
-    ways = [(ensemble.at[pl.ds(size * n, size)], ensemble_v.at[pl.ds(size * n, size)],
-             ensemble_out.at[pl.ds(size * n, size)]) for n in range(PARTS)]
-    ways.append((averages, averages_v, averages_out))
-    into = [pltpu.make_async_copy(source, middle, sem_in.at[n]) for n, (source, middle, _) in enumerate(ways)]
-    away = [pltpu.make_async_copy(middle, target, sem_out.at[n]) for n, (_, middle, target) in enumerate(ways)]
+def hand_over(ensemble, last, averages, ensemble_out, averages_out, ensemble_v, last_v, averages_v, new_v, sem_in,
+              sem_out):
+    strips = [pl.ds(STRIPS * f, STRIPS) for f in range(PAIR)]
+    into = [pltpu.make_async_copy(last.at[s], last_v.at[s], sem_in.at[f]) for f, s in enumerate(strips)]
+    into.append(pltpu.make_async_copy(ensemble, ensemble_v, sem_in.at[PAIR]))
+    into.append(pltpu.make_async_copy(averages, averages_v, sem_in.at[PAIR + 1]))
+    away = [pltpu.make_async_copy(new_v.at[f], ensemble_out.at[:, PAIR + f], sem_out.at[f]) for f in range(PAIR)]
+    away.append(pltpu.make_async_copy(ensemble_v, ensemble_out.at[:, pl.ds(0, PAIR)], sem_out.at[PAIR]))
+    away.append(pltpu.make_async_copy(averages_v, averages_out, sem_out.at[PAIR + 1]))
     for copy in into:
         copy.start()
-    for first, second in zip(into, away):
-        first.wait()
-        second.start()
+    for f in range(PAIR):
+        into[f].wait()
+
+        def loader(g):
+            return lambda u: last_v[STRIPS * f + g, :, LANES * u:LANES * (u + 1)]
+
+        for j in range(PER):
+            spans = [(WIDE * g, WIDE * j, WIDE, loader(g), PER * WIDE) for g in range(STRIPS)]
+            for u in range(COLS // LANES):
+                new_v[f, j, :, LANES * u:LANES * (u + 1)] = place(u, spans)
+        away[f].start()
+        if f == 0:
+            for n in (PAIR, PAIR + 1):
+                into[n].wait()
+                away[n].start()
     for copy in away:
         copy.wait()
 
@@ -675,12 +699,12 @@
     def vmem(*shape):
         return pltpu.VMEM(shape, f32)
 
-    scratch = [vmem(PER, FIELDS, *plane), vmem(CYCLES, FIELDS, *plane)]
+    scratch = [vmem(PER, PAIR, *plane), vmem(CYCLES, FIELDS, *plane)]
     scratch += [vmem(*a.shape) for a in operands[:4]] + [pltpu.SMEM(a.shape, a.dtype) for a in operands[4:]]
     scratch += [vmem(1, GROUPS, ROWS, PER * SPAN) for _ in range(2)]
     scratch += [vmem(GROUPS, ROWS, PER * WIDE) for _ in range(2)] + [vmem((ROWS + 1) * PAIRS, LANES)]
     scratch += [vmem(CHUNKS, GROUPS, ROWS, PER * SPAN) for _ in range(2)]
-    scratch += [vmem(CHUNKS, GROUPS, ROWS, PER * WIDE) for _ in range(2)]
+    scratch += [vmem(n, GROUPS, ROWS, PER * WIDE) for n in (CHUNKS, 1)]
     scratch += [vmem(SLOTS, PER // 2, *plane) for _ in range(4)]
     scratch += [
         vmem(SLOTS, PER, *plane),
@@ -711,6 +735,7 @@
         vmem(CHUNKS, 2, CHIPS, *one),
         pltpu.SemaphoreType.DMA((12,)),
         pltpu.SemaphoreType.DMA((CHUNKS, 2)),
+        pltpu.SemaphoreType.DMA,
         pltpu.SemaphoreType.DMA((CHUNKS, 3)),
         pltpu.SemaphoreType.DMA((CHUNKS, 3)),
         pltpu.SemaphoreType.DMA((SLOTS, 2)),
@@ -725,11 +750,12 @@
     results = pl.pallas_call(
         kernel,
         out_shape=(
-            jax.ShapeDtypeStruct((PER, FIELDS) + plane, f32),
+            jax.ShapeDtypeStruct((PER, PAIR) + plane, f32),
+            jax.ShapeDtypeStruct((GROUPS, ROWS, PER * WIDE), f32),
             jax.ShapeDtypeStruct((CYCLES, FIELDS) + plane, f32),
         ),
         in_specs=[anywhere] * 8,
-        out_specs=(anywhere, anywhere),
+        out_specs=(anywhere,) * 3,
         scratch_shapes=scratch,
         compiler_params=pltpu.CompilerParams(
             collective_id=0, has_side_effects=True, vmem_limit_bytes=60 * 1024 * 1024
@@ -738,10 +764,14 @@
     )(*operands)
     return pl.pallas_call(
         hand_over,
-        out_shape=tuple(jax.ShapeDtypeStruct(r.shape, f32) for r in results),
-        in_specs=[anywhere] * 2,
+        out_shape=(
+            jax.ShapeDtypeStruct((PER, FIELDS) + plane, f32),
+            jax.ShapeDtypeStruct((CYCLES, FIELDS) + plane, f32),
+        ),
+        in_specs=[anywhere] * 3,
         out_specs=(anywhere, anywhere),
-        scratch_shapes=[vmem(*r.shape) for r in results] + [pltpu.SemaphoreType.DMA((PARTS + 1,))] * 2,
+        scratch_shapes=[vmem(*r.shape) for r in results] + [vmem(PAIR, PER, *plane)]
+        + [pltpu.SemaphoreType.DMA((PAIR + 2,))] * 2,
         compiler_params=pltpu.CompilerParams(vmem_limit_bytes=60 * 1024 * 1024),
         name="hand_over",
     )(*results)

time: 77.7 us -> 76.7 us (0.987)
  Pallas kernels: 76.9 us -> 76 us
    pallas_call x2, Pallas kernels: 76.9 us -> 76 us  [the longest x1 73.8 us: per_device(): pl.pallas_call(kernel, out_shape=(jax.ShapeDtypeStruct((PER, PAIR) + plan...]
where the time goes in v2:
time: 76.7 us; the launch traced here: 76.6 us
  Pallas kernels  76 us (99%)
    pallas_call x1, Pallas kernels, per_device(): pl.pallas_call(kernel, out_shape=(jax.ShapeDtypeStruct((PER, PAIR) + plan...  73.8 us
    pallas_call x1, Pallas kernels, per_device(): pl.pallas_call(hand_over, out_shape=(jax.ShapeDtypeStruct((PER, FIELDS) +...  2.2 us

profile of v2, /device:TPU:1, one launch (start us, length us, event | category | flops | bytes accessed | tf_op | source)
XLA Modules:
  0.0 76.6 jit_solution(17374886430771425838)
XLA Ops:
  0.6 73.8 %assimilate.1 = (f32[16,2,8,384]{3,2,1,0:T(8,128)}, f32[16,8,768]{2,1,0:T(8,128)}, f32[2,4,8,384]{3,2,1,0:T(8,128)}) custom-call(f32[16,4,8,384]{3,2,1,0:T(8,128)} %members.1, f32[2,16,4,8,384]{4,3,2,1,0:T(8,128)} %noise.1, f32[2,8,384]{2,1,0:T(8,128)} %courant.1, f32[4,8,384]{2,1,0:T(8,128)} %diffusion.1, s32[1,64]{1,0:T(1,128)} %obs_loc.1, ...), custom_call_target="tpu_custom_call" | custom-call | tf_op jit(solution)/shard_map/assimilate/pallas_call | solution.py:750
  74.4 2.2 %hand_over.1 = (f32[16,4,8,384]{3,2,1,0:T(8,128)}, f32[2,4,8,384]{3,2,1,0:T(8,128)}) custom-call(f32[16,2,8,384]{3,2,1,0:T(8,128)} %get-tuple-element.5.ensemble, f32[16,8,768]{2,1,0:T(8,128)} %get-tuple-element.6.last, f32[2,4,8,384]{3,2,1,0:T(8,128)} %get-tuple-element.7.averages), custom_call_target="tpu_custom_call" | custom-call | tf_op jit(solution)/shard_map/hand_over/pallas_call | solution.py:765

commit v3 on v2

--- a/solution.py
+++ b/solution.py
@@ -611,12 +611,12 @@
     for block in range(BLOCKS):
         forecast2(0, block)
     likelihood2()
-    pack_back(0)
-    swap(back_send, back_recv, 0, 2)
     await_bytes(others(state_recv, 1), sem_in.at[1, 1])
     unpack_state(1)
     for block in range(BLOCKS):
         begin2(1, block)
+    pack_back(0)
+    swap(back_send, back_recv, 0, 2)
     weigh2()
     average2(0)
     average(1)

time: 76.7 us -> 76.1 us (level)
  no operation moved by 1% of the time
where the time goes in v3:
time: 76.1 us; the launch traced here: 76 us
  Pallas kernels  75.3 us (99%)
    pallas_call x1, Pallas kernels, per_device(): pl.pallas_call(kernel, out_shape=(jax.ShapeDtypeStruct((PER, PAIR) + plan...  73.1 us
    pallas_call x1, Pallas kernels, per_device(): pl.pallas_call(hand_over, out_shape=(jax.ShapeDtypeStruct((PER, FIELDS) +...  2.2 us

profile of v3, /device:TPU:1, one launch (start us, length us, event | category | flops | bytes accessed | tf_op | source)
XLA Modules:
  0.0 76.0 jit_solution(16452965832298740602)
XLA Ops:
  0.6 73.1 %assimilate.1 = (f32[16,2,8,384]{3,2,1,0:T(8,128)}, f32[16,8,768]{2,1,0:T(8,128)}, f32[2,4,8,384]{3,2,1,0:T(8,128)}) custom-call(f32[16,4,8,384]{3,2,1,0:T(8,128)} %members.1, f32[2,16,4,8,384]{4,3,2,1,0:T(8,128)} %noise.1, f32[2,8,384]{2,1,0:T(8,128)} %courant.1, f32[4,8,384]{2,1,0:T(8,128)} %diffusion.1, s32[1,64]{1,0:T(1,128)} %obs_loc.1, ...), custom_call_target="tpu_custom_call" | custom-call | tf_op jit(solution)/shard_map/assimilate/pallas_call | solution.py:750
  73.8 2.2 %hand_over.1 = (f32[16,4,8,384]{3,2,1,0:T(8,128)}, f32[2,4,8,384]{3,2,1,0:T(8,128)}) custom-call(f32[16,2,8,384]{3,2,1,0:T(8,128)} %get-tuple-element.5.ensemble, f32[16,8,768]{2,1,0:T(8,128)} %get-tuple-element.6.last, f32[2,4,8,384]{3,2,1,0:T(8,128)} %get-tuple-element.7.averages), custom_call_target="tpu_custom_call" | custom-call | tf_op jit(solution)/shard_map/hand_over/pallas_call | solution.py:765
